TPU v7x, 32 devices: a whole 2x2x4 slice. The times are simulated.
32 devices in a mesh: groups: 2 (over x), wide: 8 (over z, y), narrow: 2 (over core).
Axes of the slice: x: 2, y: 2, z: 4, core: 2. Of those that a mesh axis runs over, the one named last changes fastest.
Arguments:
- activations: bfloat16 [256, 5120], P(('groups', 'narrow'), 'wide'), parts along dimension 0, may hold values from -6 to 6
- out_grads: bfloat16 [256, 25600], P(('groups', 'wide'), 'narrow'), parts along dimension 0, may hold values from -0.029907227 to 0.029907227
- second_moment: float32 [5120, 25600], P('wide', 'narrow'), may hold values from 0.0001 to 0.01
- seq_ids: int32 [256], P('groups'), parts along dimension 0, may hold values from 0 to 1, never falling along the last dimension, each value on 1 to 96 neighbouring positions
- seed_word: int32 [1], replicated, may hold values from 0 to 1073741823
- row_keys: int32 [5120], P('wide'), may hold values from 0 to 1073741823
- col_keys: int32 [25600], P('narrow'), may hold values from 0 to 1073741823
Outputs:
- features: float32 [4, 1024], P('groups'), parts along dimension 0
There are 2 independent parts, one for each index of `groups`. A program takes and returns all parts, laid end to end along the dimension named above; an argument that names none is the same for every part. Nothing has to cross between parts.
Inputs may be any that keep to these rules, and one draw needn't show every extreme that they name: `seq_ids`: tokens of one sequence stand together, sequence numbers never fall along the tokens, and every sequence has at least one token.
All inputs are finite; a program needn't handle non-finite values.
Results may differ from a plain program's by a relative error of at most 0.0029.
Values may be sent and summed in bfloat16 or wider, within the bound.
A program may use at most 192 MiB of HBM per device.

v0:
```python
import jax
import jax.numpy as jnp
from jax import lax
from jax.sharding import PartitionSpec as P

D = 5120
FF = 25600
K = 1024
SEQS = 2


adam_epsilon = 1e-08


def scramble(number):
    number = number * 668265261
    number = number ^ lax.shift_right_logical(number, jnp.full_like(number, 15))
    number = number * 739982445
    number = number ^ lax.shift_right_logical(number, jnp.full_like(number, 13))
    number = number * 695872825
    return number ^ lax.shift_right_logical(number, jnp.full_like(number, 16))


def rademacher(key_list, seed_word, salt_value, count_cols):
    salted = scramble(key_list ^ seed_word[0] + salt_value)
    columns = lax.broadcasted_iota(jnp.int32, (key_list.shape[0], count_cols), 1)
    hashed = scramble(salted[:, None] ^ scramble(columns + salt_value))
    parity = lax.shift_right_logical(hashed, jnp.full_like(hashed, 20)) & 1
    return (1 - 2 * parity).astype(jnp.float32)


def on_device(activations, out_grads, second_moment, seq_ids, seed_word, row_keys, col_keys):
    whole_x = lax.all_gather(activations, "narrow", axis=0, tiled=True)
    local_rows = second_moment.shape[0]
    row_signs = rademacher(row_keys, seed_word, 1, K)
    col_signs = rademacher(col_keys, seed_word, 2, K).astype(jnp.bfloat16)
    precond = 1.0 / (jnp.sqrt(second_moment) + adam_epsilon)
    whole_dy = lax.all_gather(out_grads, "wide", axis=0, tiled=True)
    grad_list = []
    for segment in range(SEQS):
        picked = jnp.where((seq_ids == segment)[:, None], whole_x, jnp.zeros_like(whole_x))
        grad_list.append(jnp.dot(picked.T, whole_dy, preferred_element_type=jnp.float32))
    stacked = jnp.concatenate([(grad * precond).astype(jnp.bfloat16) for grad in grad_list], axis=0)
    mapped = jnp.dot(stacked, col_signs, preferred_element_type=jnp.float32).reshape(
        SEQS, local_rows, K
    )
    norm_factor = 1.0 / jnp.sqrt(jnp.float32(D) * jnp.float32(FF))
    partial_value = jnp.sum(mapped * row_signs[None], axis=1) * norm_factor
    paired = lax.psum(partial_value, "narrow")
    features = lax.psum(paired, "wide")
    return features


def solution(mesh):
    placed = (
        P(("groups", "narrow"), "wide"),
        P(("groups", "wide"), "narrow"),
        P("wide", "narrow"),
        P("groups"),
        P(),
        P("wide"),
        P("narrow"),
    )
    return jax.shard_map(
        on_device, mesh=mesh, in_specs=placed, out_specs=P("groups", None), check_vma=False
    )
```

profile of v0, /device:TPU:0, one launch (start us, length us, event | category | flops | bytes accessed | tf_op | source)
XLA Modules:
  0.0 231.8 jit_solution(4927974159132249378)
XLA Ops:
  6.5 0.0 all-gather.2.cloned.1.call-start
  6.5 0.7 all-gather.2.cloned.1.call-update
  7.9 2.2 all_gather.6
  10.2 0.7 broadcast_compare_fusion.1
  10.8 0.7 shift-right-logical_xor_fusion.12
  11.5 2.8 %fusion.30 = f32[640,1024]{1,0:T(8,128)} fusion(s32[1024]{0:T(1024)S(1)} %shift-right-logical_xor_fusion.9, s32[640]{0:T(1024)S(1)} %shift-right-logical_xor_fusion.12), kind=kLoop, calls=%fused_computation.39 | loop fusion | flops 9830400 | bytes 2628096 | tf_op jit(solution)/shard_map/convert_element_type | solution.py:29
  14.4 0.8 shift-right-logical_xor_fusion.6
  15.2 59.1 %all-gather.2.cloned.1.call-done = bf16[128,12800]{1,0:T(8,128)(2,1)} async-done(((bf16[16,12800]{1,0:T(8,128)(2,1)}), bf16[128,12800]{1,0:T(8,128)(2,1)}) %all-gather.2.cloned.1.call-update) | async-done | bytes 3276816 | tf_op jit(solution)/shard_map/all_gather | solution.py:38
  74.2 0.0 copy-start.1
  74.3 25.0 %multiply_convert_fusion = bf16[640,12800]{1,0:T(8,128)(2,1)} fusion(bf16[128,12800]{1,0:T(8,128)(2,1)} %all-gather.2.cloned.1.call-done, f32[640,12800]{1,0:T(8,128)} %param.9, bf16[128,640]{1,0:T(8,128)(2,1)S(1)} %all_gather.6, pred[128]{0:T(512)(128)(4,1)S(1)} %get-tuple-element.6), kind=kOutput, calls=%fused_computation.15 | convolution fusion | flops 2130001920 | bytes 52592768 | tf_op jit(solution)/shard_map/dot_general | solution.py:42
  99.2 0.0 copy-done.1
  99.2 20.8 %multiply_convert_fusion.1 = bf16[640,12800]{1,0:T(8,128)(2,1)} fusion(bf16[128,12800]{1,0:T(8,128)(2,1)S(1)} %copy-done.1, f32[640,12800]{1,0:T(8,128)} %param.9, bf16[128,640]{1,0:T(8,128)(2,1)S(1)} %all_gather.6, pred[128]{0:T(512)(128)(4,1)S(1)} %get-tuple-element.5), kind=kOutput, calls=%fused_computation.16 | convolution fusion | flops 2130001920 | bytes 52592768 | tf_op jit(solution)/shard_map/dot_general | solution.py:42
  120.0 0.0 copy-start
  120.0 81.5 %fusion.8 = f32[1280,1024]{1,0:T(8,128)S(1)} fusion(bf16[640,12800]{1,0:T(8,128)(2,1)} %multiply_convert_fusion, bf16[640,12800]{1,0:T(8,128)(2,1)} %multiply_convert_fusion.1, s32[1024]{0:T(1024)S(1)} %shift-right-logical_xor_fusion.15, s32[12800]{0:T(1024)S(1)} %shift-right-logical_xor_fusion.6), kind=kOutput, calls=%fused_computation.11 | convolution fusion | flops 33829683200 | bytes 38066176 | tf_op jit(solution)/shard_map/dot_general | solution.py:44
  201.6 0.0 copy-done
  201.6 1.1 multiply_reduce_fusion
  202.7 2.5 %psum.14 = f32[2,1024]{1,0:T(2,128)S(1)} all-reduce(f32[2,1024]{1,0:T(2,128)S(1)} %broadcast_multiply_fusion), channel_id=1, replica_groups=mesh['groups'=2,'wide'=8,'narrow'=2] {'narrow'}, use_global_device_ids=true, to_apply=%region_1.2 | all-reduce | flops 2048 | bytes 16384 | tf_op jit(solution)/shard_map/psum | solution.py:49
  205.2 19.8 %psum.15 = f32[2,1024]{1,0:T(2,128)} all-reduce(f32[2,1024]{1,0:T(2,128)S(1)} %psum.14), channel_id=1, replica_groups=mesh['groups'=2,'wide'=8,'narrow'=2] {'wide'}, use_global_device_ids=true, to_apply=%region_2.3 | all-reduce | flops 2048 | bytes 16384 | tf_op jit(solution)/shard_map/psum | solution.py:50
  (3 shorter events, 0.0 us)
Async XLA Ops:
  6.5 67.7 %all-gather.2.cloned.1.call-start = ((), (), s32[]{:S(2)}) async-start(), calls=%async_computation | async-start | bytes 3686400 | tf_op jit(solution)/shard_map/all_gather | solution.py:38
  74.2 25.0 %copy-start.1 = (bf16[128,12800]{1,0:T(8,128)(2,1)S(1)}, bf16[128,12800]{1,0:T(8,128)(2,1)}, u32[]{:S(2)}) copy-start(bf16[128,12800]{1,0:T(8,128)(2,1)} %all-gather.2.cloned.1.call-done) | copy-start | bytes 9830404
  120.0 81.5 %copy-start = (f32[640,1024]{1,0:T(8,128)S(1)}, f32[640,1024]{1,0:T(8,128)}, u32[]{:S(2)}) copy-start(f32[640,1024]{1,0:T(8,128)} %fusion.30) | copy-start | bytes 7864324
Sparse Core Ops, SparseCore 0:
  9.5 64.6 all-gather.1
where the time goes:
time: 232 us
  matrix products  127 us (55%)
  waiting for transfers between devices  59.8 us (26%)
  blocking collectives  24.5 us (11%)
  between operations  14.1 us (6%)
  other arithmetic  6.14 us (3%)
    dot_general x1, matrix products, on_device(): jnp.dot(stacked, col_signs, preferred_element_type=jnp.float32)  81.5 us
    all_gather x1, waiting for transfers between devices, on_device(): whole_dy = lax.all_gather(out_grads, 'wide', axis=0, tiled=True)  59.1 us
    dot_general x2, matrix products, on_device(): jnp.dot(picked.T, whole_dy, preferred_element_type=jnp.float32)  45.8 us
    psum x1, blocking collectives, on_device(): features = lax.psum(paired, 'wide')  19.8 us
  transfers between devices with their start and end apart: 1, of which 1 were waited for; matrix products, arithmetic and copies ran while one was open for 2% of the time, Pallas kernels for 0%

commit v1 on v0

v1 whole, which is shorter than its diff:
```python
import functools

import jax
import jax.numpy as jnp
from jax import lax
from jax.experimental import pallas as pl
from jax.experimental.pallas import tpu as pltpu
from jax.sharding import PartitionSpec as P

D = 5120
FF = 25600
K = 1024
SEQS = 2

adam_epsilon = 1e-08
PIECES = (1, 2, 2)


def scramble_start(number):
    number = number * 668265261
    number = number ^ lax.shift_right_logical(number, jnp.full_like(number, 15))
    number = number * 739982445
    return number ^ lax.shift_right_logical(number, jnp.full_like(number, 13))


def scramble(number):
    number = scramble_start(number) * 695872825
    return number ^ lax.shift_right_logical(number, jnp.full_like(number, 16))


LAST = ((695872825 << 11) + (1 << 31)) % (1 << 32) - (1 << 31)


def signs_of(salted, lanes):
    mixed = scramble_start(salted ^ lanes) * LAST
    return jnp.where(mixed < 0, jnp.float32(-1.0), jnp.float32(1.0))


def prepare_kernel(first_ref, salted_ref, lanes_ref, moment_ref, signs_ref, precond_ref, *, step):
    def hash_rows(i, carry):
        rows = pl.ds(pl.multiple_of(i * step, step), step)
        signs_ref[rows, :] = signs_of(salted_ref[rows, :], lanes_ref[...]).astype(jnp.bfloat16)
        return carry

    lax.fori_loop(0, signs_ref.shape[0] // step, hash_rows, 0)

    def moment_rows(i, carry):
        rows = pl.ds(pl.multiple_of(i * 8, 8), 8)
        precond_ref[rows, :] = 1.0 / (jnp.sqrt(moment_ref[rows, :]) + adam_epsilon)
        return carry

    lax.fori_loop(0, moment_ref.shape[0] // 8, moment_rows, 0)


def map_kernel(picked_ref, dy_ref, precond_ref, signs_ref, salted_ref, lanes_ref, out_ref, rows_ref):
    rows = precond_ref.shape[0]

    @pl.when(pl.program_id(0) == 0)
    def _():
        out_ref[...] = jnp.zeros_like(out_ref)

        def hash_rows(i, carry):
            part = pl.ds(pl.multiple_of(i * 8, 8), 8)
            rows_ref[part, :] = signs_of(salted_ref[part, :], lanes_ref[...])
            return carry

        lax.fori_loop(0, rows // 8, hash_rows, 0)

    for s in range(picked_ref.shape[0]):
        grad = jnp.dot(picked_ref[s], dy_ref[...], preferred_element_type=jnp.float32)
        scaled = (grad * precond_ref[...]).astype(jnp.bfloat16)
        mapped = jnp.dot(scaled, signs_ref[...], preferred_element_type=jnp.float32)
        out_ref[s : s + 1, :] += jnp.sum(mapped * rows_ref[...], axis=0, keepdims=True)


def on_device(activations, out_grads, second_moment, seq_ids, seed_word, row_keys, col_keys):
    groups = lax.axis_size("groups")
    wide = lax.axis_size("wide")
    me = lax.axis_index("groups")
    rows, all_cols = second_moment.shape
    cols = all_cols // groups
    tokens = seq_ids.shape[0]
    per = out_grads.shape[0]
    chunk = 1280 if cols % 1280 == 0 else 640
    count = cols // chunk

    with jax.named_scope("exchange"):
        parts = [lax.dynamic_slice_in_dim(out_grads, me * cols, cols, axis=1)]
        for shift in range(1, groups):
            target = lax.rem(me + shift, groups)
            block = lax.dynamic_slice_in_dim(out_grads, target * cols, cols, axis=1)
            parts.append(lax.ppermute(block, "groups", [(i, (i + shift) % groups) for i in range(groups)]))
        mine = jnp.concatenate(parts, axis=0)

    pieces, start = [], 0
    for size in PIECES:
        if start < count:
            pieces.append((start, min(size, count - start)))
            start += size
    if start < count:
        pieces.append((start, count - start))

    gathered = []
    for at, size in pieces:
        piece = mine[:, at * chunk : (at + size) * chunk]
        gathered.append(lax.all_gather(piece, "wide", axis=0, tiled=True))

    with jax.named_scope("masked_activations"):
        whole_x = lax.all_gather(activations, ("groups", "narrow"), axis=0, tiled=True)
        ids = lax.all_gather(seq_ids, "groups", axis=0, tiled=True).reshape(groups, wide, per)
        order = lax.rem(me + groups - jnp.arange(groups), groups)
        x = jnp.take(whole_x.reshape(groups, wide, per, rows), order, axis=0)
        ids = jnp.take(ids, order, axis=0)
        x = x.transpose(3, 1, 0, 2).reshape(rows, groups * tokens)
        which = ids + SEQS * jnp.arange(groups, dtype=jnp.int32)[:, None, None]
        which = which.transpose(1, 0, 2).reshape(groups * tokens)
        mask = which[None, :] == jnp.arange(groups * SEQS, dtype=jnp.int32)[:, None]
        picked = jnp.where(mask[:, None, :], x[None], jnp.zeros_like(x)[None])

    seed = seed_word[0]
    lane = jnp.arange(K, dtype=jnp.int32)[None, :]
    row_salted = scramble(row_keys ^ (seed + 1))[:, None]
    my_keys = lax.dynamic_slice_in_dim(col_keys, me * cols, cols)
    col_salted = scramble(my_keys ^ (seed + 2))[:, None]
    row_lanes = scramble(lane + 1)
    col_lanes = scramble(lane + 2)

    signs, precond = pl.pallas_call(
        functools.partial(prepare_kernel, step=16),
        grid_spec=pltpu.PrefetchScalarGridSpec(
            num_scalar_prefetch=1,
            grid=(count,),
            in_specs=[
                pl.BlockSpec((chunk, 1), lambda i, f: (i, 0)),
                pl.BlockSpec((1, K), lambda i, f: (0, 0)),
                pl.BlockSpec((rows, chunk), lambda i, f: (0, f[0] + i)),
            ],
            out_specs=[
                pl.BlockSpec((chunk, K), lambda i, f: (i, 0)),
                pl.BlockSpec((rows, chunk), lambda i, f: (0, i)),
            ],
        ),
        out_shape=[
            jax.ShapeDtypeStruct((cols, K), jnp.bfloat16),
            jax.ShapeDtypeStruct((rows, cols), jnp.float32),
        ],
        compiler_params=pltpu.CompilerParams(vmem_limit_bytes=40 << 20),
        cost_estimate=pl.CostEstimate(flops=cols * K * 20, bytes_accessed=rows * cols * 8 + cols * K * 2, transcendentals=2 * rows * cols),
        name="prepare",
    )((me * count).astype(jnp.int32).reshape(1), col_salted, col_lanes, second_moment)

    total = jnp.zeros((groups * SEQS, K), jnp.float32)
    for (at, size), dy in zip(pieces, gathered):
        total = total + pl.pallas_call(
            map_kernel,
            grid=(size,),
            in_specs=[
                pl.BlockSpec(picked.shape, lambda i: (0, 0, 0)),
                pl.BlockSpec((dy.shape[0], chunk), lambda i: (0, i)),
                pl.BlockSpec((rows, chunk), lambda i, at=at: (0, at + i)),
                pl.BlockSpec((chunk, K), lambda i, at=at: (at + i, 0)),
                pl.BlockSpec((rows, 1), lambda i: (0, 0)),
                pl.BlockSpec((1, K), lambda i: (0, 0)),
            ],
            out_specs=pl.BlockSpec((groups * SEQS, K), lambda i: (0, 0)),
            out_shape=jax.ShapeDtypeStruct((groups * SEQS, K), jnp.float32),
            scratch_shapes=[pltpu.VMEM((rows, K), jnp.float32)],
            compiler_params=pltpu.CompilerParams(vmem_limit_bytes=56 << 20),
            cost_estimate=pl.CostEstimate(
                flops=2 * groups * SEQS * rows * size * chunk * (K + 256),
                bytes_accessed=size * chunk * (rows * 4 + K * 2),
                transcendentals=0,
            ),
            name="map_piece",
        )(picked, dy, precond, signs, row_salted, row_lanes)

    with jax.named_scope("reduce"):
        norm_factor = 1.0 / jnp.sqrt(jnp.float32(D) * jnp.float32(FF))
        total = total.reshape(groups, SEQS, K) * norm_factor
        features = total[0]
        for e in range(1, groups):
            features = features + lax.ppermute(total[e], "groups", [(i, (i - e) % groups) for i in range(groups)])
        return lax.psum(features, ("wide", "narrow"))


def solution(mesh):
    placed = (
        P(("groups", "narrow"), "wide"),
        P(("groups", "wide"), "narrow"),
        P("wide", "narrow"),
        P("groups"),
        P(),
        P("wide"),
        P("narrow"),
    )
    return jax.shard_map(
        on_device, mesh=mesh, in_specs=placed, out_specs=P("groups", None), check_vma=False
    )
```

time: 232 us -> 246 us (1.060)
  Pallas kernels: 0 us -> 129 us
  matrix products: 127 us -> 0 us
  waiting for transfers between devices: 59.8 us -> 6.74 us
  blocking collectives: 24.5 us -> 76.8 us
  local copies, waits for them, and re-layouts: 0.01 us -> 9.06 us
  starting transfers between devices: 0.01 us -> 3.62 us
    pallas_call x0 -> x4, Pallas kernels: none -> 129 us  [the longest x3 77 us: on_device(): pl.pallas_call(map_kernel, grid=(size,), in_specs=[pl.BlockSpec(picked.sh...]
    dot_general x3 -> x0, matrix products: 127 us -> none  [the longest x1 81.5 us: on_device(): jnp.dot(stacked, col_signs, preferred_element_type=jnp.float32)]
    all_gather x1 -> x2, waiting for transfers between devices: 59.1 us -> 0.01 us  [on_device(): gathered.append(lax.all_gather(piece, 'wide', axis=0, tiled=True))]
    all_gather x1 -> x3, blocking collectives: 2.23 us -> 46.2 us  [the longest x1 34.1 us: on_device(): gathered.append(lax.all_gather(piece, 'wide', axis=0, tiled=True))]
    psum x2 -> x1, blocking collectives: 22.3 us -> 30.6 us  [on_device(): return lax.psum(features, ('wide', 'narrow'))]
    ppermute x0 -> x2, waiting for transfers between devices: none -> 6.69 us  [the longest x1 3.55 us: on_device(): lax.ppermute(block, 'groups', [(i, (i + shift) % groups) for i in range(g...]
    broadcast_in_dim x0 -> x3, local copies, waits for them, and re-layouts: none -> 3.66 us  [the longest x1 1.86 us: on_device(): picked = jnp.where(mask[:, None, :], x[None], jnp.zeros_like(x)[None])]
    ppermute x0 -> x2, starting transfers between devices: none -> 3.58 us  [the longest x1 3 us: on_device(): lax.ppermute(block, 'groups', [(i, (i + shift) % groups) for i in range(g...]
  transfers between devices with their start and end apart: 1 -> 4, of which waited for: 1 -> 2; matrix products, arithmetic and copies ran while one was open for 2% -> 5% of each run, Pallas kernels for 0% -> 41%
where the time goes in v1:
time: 246 us; the launch traced here: 245 us
  Pallas kernels  129 us (52%)
  blocking collectives  76.8 us (31%)
  between operations  14.2 us (6%)
  local copies, waits for them, and re-layouts  9.06 us (4%)
  waiting for transfers between devices  6.74 us (3%)
  other arithmetic  6.1 us (2%)
  starting transfers between devices  3.62 us (1%)
    pallas_call x3, Pallas kernels, on_device(): pl.pallas_call(map_kernel, grid=(size,), in_specs=[pl.BlockSpec(picked.sh...  77 us
    pallas_call x1, Pallas kernels, on_device(): pl.pallas_call(functools.partial(prepare_kernel, step=16), grid_spec=pltp...  51.8 us
    all_gather x1, blocking collectives, on_device(): gathered.append(lax.all_gather(piece, 'wide', axis=0, tiled=True))  34.1 us
    psum x1, blocking collectives, on_device(): return lax.psum(features, ('wide', 'narrow'))  30.6 us
    all_gather x1, blocking collectives, on_device(): lax.all_gather(activations, ('groups', 'narrow'), axis=0, tiled=True)  7.84 us
  transfers between devices with their start and end apart: 4, of which 2 were waited for; matrix products, arithmetic and copies ran while one was open for 5% of the time, Pallas kernels for 41%

profile of v1, /device:TPU:0, one launch (start us, length us, event | category | flops | bytes accessed | tf_op | source)
XLA Modules:
  0.0 245.2 jit_solution(17228968323800486156)
XLA Ops:
  6.5 0.0 all-gather.4.cloned.1.call-start
  6.5 1.1 constant_dynamic-slice_fusion.1
  7.6 3.0 %collective-permute-start = (bf16[16,6400]{1,0:T(8,128)(2,1)S(1)}, bf16[16,6400]{1,0:T(8,128)(2,1)S(1)}, u32[]{:S(2)}, u32[]{:S(2)}) collective-permute-start(bf16[16,6400]{1,0:T(8,128)(2,1)S(1)} %get-tuple-element.12), channel_id=1, source_target_pairs={{0,16},{16,0},{1,17},{17,1},{2,18},{18,2},{3,19},{19,3},{4,20},{20... | collective-permute-start | bytes 614408 | tf_op jit(solution)/shard_map/exchange/ppermute | solution.py:92
  11.3 0.9 shift-right-logical_xor_fusion
  12.1 3.5 %collective-permute-done = bf16[16,6400]{1,0:T(8,128)(2,1)S(1)} collective-permute-done((bf16[16,6400]{1,0:T(8,128)(2,1)S(1)}, bf16[16,6400]{1,0:T(8,128)(2,1)S(1)}, u32[]{:S(2)}, u32[]{:S(2)}) %collective-permute-start) | collective-permute-done | bytes 204832 | tf_op jit(solution)/shard_map/exchange/ppermute | solution.py:92
  15.7 0.0 copy-start.1
  15.7 0.8 pad_maximum_fusion.1
  16.5 0.0 all-gather.4.cloned.1.call-update
  16.5 0.0 all-gather.6.cloned.1.call-start
  16.6 0.0 copy-done.1
  16.6 0.9 broadcast_in_dim.91.salted_ref
  17.5 7.8 %all_gather.16 = bf16[256,640]{1,0:T(8,128)(2,1)} all-gather(bf16[64,640]{1,0:T(8,128)(2,1)} %param.7), channel_id=1, replica_groups=mesh['groups'=2,'wide'=8,'narrow'=2] {'groups','narrow'}, dimensions={0}, use_global_device_ids=true | all-gather | bytes 409600 | tf_op jit(solution)/shard_map/masked_activations/all_gather | solution.py:109
  25.4 0.0 copy-start.6
  25.4 0.0 copy-start.5
  25.4 2.3 gather_fusion.1
  27.7 1.1 select_bitcast_fusion
  28.8 0.8 copy.22
  29.5 1.9 copy.23
  31.4 0.0 copy-done.6
  31.4 4.2 %all-gather = s32[2,1,128]{2,1,0:T(1,128)S(1)} all-gather(s32[1,1,128]{2,1,0:T(1,128)S(1)} %bitcast.14), channel_id=1, replica_groups=mesh['groups'=2,'wide'=8,'narrow'=2] {'groups'}, dimensions={0}, use_global_device_ids=true | all-gather | bytes 1536 | tf_op jit(solution)/shard_map/masked_activations/all_gather | solution.py:110
  35.6 0.5 broadcast.276
  36.1 0.7 reduce.3
  36.8 0.1 reshape.175
  36.8 0.6 gather_fusion
  37.4 0.1 add_bitcast_fusion
  37.5 0.1 eq.19
  37.6 0.0 copy-done.5
  37.6 0.9 broadcast_in_dim.92.salted_ref
  38.5 0.0 copy-start
  38.5 51.8 %prepare.1 = (bf16[6400,1024]{1,0:T(8,128)(2,1)}, f32[640,6400]{1,0:T(8,128)}) custom-call(s32[1]{0:T(128)} %bitcast.6.first_ref, s32[6400,1]{1,0:T(8,128)S(1)} %broadcast_in_dim.91.salted_ref, s32[1,1024]{1,0:T(1,128)S(1)} %shift-right-logical_xor_fusion.9.lanes_ref, f32[640,12800]{1,0:T(8,128)} %moment_ref.1), custom_call_target="tpu_custom_call" | custom-call | flops 131072000 | bytes 45875200 | tf_op jit(solution)/shard_map/prepare/pallas_call | solution.py:128
  90.3 0.0 copy-start.2
  90.3 0.6 shift-right-logical_xor_fusion.3.lanes_ref
  90.9 0.0 copy-done
  90.9 1.2 broadcast_select_fusion.picked_ref
  92.1 0.0 copy-done.2
  92.1 34.1 %all_gather.17.dy_ref = bf16[256,1280]{1,0:T(8,128)(2,1)} all-gather(bf16[32,1280]{1,0:T(8,128)(2,1)S(1)} %pad_maximum_fusion.2), channel_id=1, replica_groups=mesh['groups'=2,'wide'=8,'narrow'=2] {'wide'}, dimensions={0}, use_global_device_ids=true | all-gather | bytes 737280 | tf_op jit(solution)/shard_map/all_gather | solution.py:106
  126.3 0.0 all-gather.6.cloned.1.call-update
  126.3 19.1 %map_piece.3 = f32[4,1024]{1,0:T(4,128)} custom-call(bf16[4,640,256]{2,1,0:T(8,128)(2,1)} %broadcast_select_fusion.picked_ref, bf16[256,1280]{1,0:T(8,128)(2,1)} %all_gather.17.dy_ref, f32[640,6400]{1,0:T(8,128)} %get-tuple-element.7.precond_ref, bf16[6400,1024]{1,0:T(8,128)(2,1)} %get-tuple-element.8.signs_ref, s32[640,1]{1,0:T(8,128)} %broadcast_in_dim.92.salted_ref, ...), custom_call_target="tpu_custom_call" | custom-call | flops 8388608000 | bytes 5898240 | tf_op jit(solution)/shard_map/map_piece/pallas_call | solution.py:154
  145.4 0.0 all-gather.4.cloned.1.call-done.dy_ref
  145.4 28.9 %map_piece.4 = f32[4,1024]{1,0:T(4,128)} custom-call(bf16[4,640,256]{2,1,0:T(8,128)(2,1)} %broadcast_select_fusion.picked_ref, bf16[256,2560]{1,0:T(8,128)(2,1)} %all-gather.4.cloned.1.call-done.dy_ref, f32[640,6400]{1,0:T(8,128)} %get-tuple-element.7.precond_ref, bf16[6400,1024]{1,0:T(8,128)(2,1)} %get-tuple-element.8.signs_ref, ...), custom_call_target="tpu_custom_call" | custom-call | flops 16777216000 | bytes 11796480 | tf_op jit(solution)/shard_map/map_piece/pallas_call | solution.py:154
  174.3 0.0 copy-start.3
  174.3 0.0 copy-start.4
  174.3 0.0 all-gather.6.cloned.1.call-done.dy_ref
  174.3 29.0 %map_piece.5 = f32[4,1024]{1,0:T(4,128)} custom-call(bf16[4,640,256]{2,1,0:T(8,128)(2,1)} %broadcast_select_fusion.picked_ref, bf16[256,2560]{1,0:T(8,128)(2,1)} %all-gather.6.cloned.1.call-done.dy_ref, f32[640,6400]{1,0:T(8,128)} %get-tuple-element.7.precond_ref, bf16[6400,1024]{1,0:T(8,128)(2,1)} %get-tuple-element.8.signs_ref, ...), custom_call_target="tpu_custom_call" | custom-call | flops 16777216000 | bytes 11796480 | tf_op jit(solution)/shard_map/map_piece/pallas_call | solution.py:154
  203.3 0.0 copy-done.3
  203.3 0.0 copy-done.4
  203.3 0.7 add_multiply_fusion
  204.1 0.6 collective-permute-start.1
  204.7 3.1 %collective-permute-done.1 = f32[2,1024]{1,0:T(2,128)S(1)} collective-permute-done((f32[2,1024]{1,0:T(2,128)S(1)}, f32[2,1024]{1,0:T(2,128)S(1)}, u32[]{:S(2)}, u32[]{:S(2)}) %collective-permute-start.1) | collective-permute-done | bytes 8224 | tf_op jit(solution)/shard_map/reduce/ppermute | solution.py:182
  207.8 30.6 %psum.7 = f32[2,1024]{1,0:T(2,128)} all-reduce(f32[2,1024]{1,0:T(2,128)S(1)} %slice_add_fusion), channel_id=1, replica_groups=mesh['groups'=2,'wide'=8,'narrow'=2] {'wide','narrow'}, use_global_device_ids=true, to_apply=%region_0.1 | all-reduce | flops 2048 | bytes 16384 | tf_op jit(solution)/shard_map/reduce/psum | solution.py:183
  (11 shorter events, 0.1 us)
Async XLA Ops:
  6.5 138.8 %all-gather.4.cloned.1.call-start = ((), (), s32[]{:S(2)}) async-start(), calls=%async_computation | async-start | bytes 1474560 | tf_op jit(solution)/shard_map/all_gather | solution.py:106
  7.6 8.1 %collective-permute-start = (bf16[16,6400]{1,0:T(8,128)(2,1)S(1)}, bf16[16,6400]{1,0:T(8,128)(2,1)S(1)}, u32[]{:S(2)}, u32[]{:S(2)}) collective-permute-start(bf16[16,6400]{1,0:T(8,128)(2,1)S(1)} %get-tuple-element.12), channel_id=1, source_target_pairs={{0,16},{16,0},{1,17},{17,1},{2,18},{18,2},{3,19},{19,3},{4,20},{20... | collective-permute-start | bytes 614408 | tf_op jit(solution)/shard_map/exchange/ppermute | solution.py:92
  15.7 0.9 copy-start.1
  16.5 157.8 %all-gather.6.cloned.1.call-start = ((), (), s32[]{:S(2)}) async-start(), calls=%async_computation.1 | async-start | bytes 1474560 | tf_op jit(solution)/shard_map/all_gather | solution.py:106
  25.4 6.0 %copy-start.6 = (s32[128]{0:T(128)S(1)}, s32[128]{0:T(128)}, u32[]{:S(2)}) copy-start(s32[128]{0:T(128)} %param.10) | copy-start | bytes 1540
  25.4 12.2 %copy-start.5 = (s32[640]{0:T(1024)S(1)}, s32[640]{0:T(1024)}, u32[]{:S(2)}) copy-start(s32[640]{0:T(1024)} %param.12) | copy-start | bytes 7684
  38.5 52.4 %copy-start = (bf16[640,256]{1,0:T(8,128)(2,1)S(1)}, bf16[640,256]{1,0:T(8,128)(2,1)}, u32[]{:S(2)}) copy-start(bf16[640,256]{1,0:T(8,128)(2,1)} %copy.23) | copy-start | bytes 983044
  90.3 1.8 copy-start.2
  174.3 29.0 %copy-start.3 = (f32[4,1024]{1,0:T(4,128)S(1)}, f32[4,1024]{1,0:T(4,128)}, u32[]{:S(2)}) copy-start(f32[4,1024]{1,0:T(4,128)} %map_piece.3) | copy-start | bytes 49156
  174.3 29.0 %copy-start.4 = (f32[4,1024]{1,0:T(4,128)S(1)}, f32[4,1024]{1,0:T(4,128)}, u32[]{:S(2)}) copy-start(f32[4,1024]{1,0:T(4,128)} %map_piece.4) | copy-start | bytes 49156
  204.1 3.7 %collective-permute-start.1 = (f32[2,1024]{1,0:T(2,128)S(1)}, f32[2,1024]{1,0:T(2,128)S(1)}, u32[]{:S(2)}, u32[]{:S(2)}) collective-permute-start(f32[2,1024]{1,0:T(2,128)S(1)} %slice.27), channel_id=1, source_target_pairs={{0,16},{16,0},{1,17},{17,1},{2,18},{18,2},{3,19},{19,3},{4,20},{20... | collective-permute-start | bytes 24584 | tf_op jit(solution)/shard_map/reduce/ppermute | solution.py:182
Sparse Core Ops, SparseCore 0:
  16.7 43.2 all-gather.3
  126.4 42.0 all-gather.5

commit v2 on v0

v2 whole, which is shorter than its diff:
```python
import functools

import jax
import jax.numpy as jnp
from jax import lax
from jax.experimental import pallas as pl
from jax.experimental.pallas import tpu as pltpu
from jax.sharding import PartitionSpec as P

D = 5120
FF = 25600
K = 1024
SEQS = 2

adam_epsilon = 1e-08
MESH = pl.DeviceIdType.MESH


def scramble_start(number):
    number = number * 668265261
    number = number ^ lax.shift_right_logical(number, jnp.full_like(number, 15))
    number = number * 739982445
    return number ^ lax.shift_right_logical(number, jnp.full_like(number, 13))


def scramble(number):
    number = scramble_start(number) * 695872825
    return number ^ lax.shift_right_logical(number, jnp.full_like(number, 16))


LAST = ((695872825 << 11) + (1 << 31)) % (1 << 32) - (1 << 31)


def signs_of(salted, lanes):
    mixed = scramble_start(salted ^ lanes) * LAST
    return jnp.where(mixed < 0, jnp.float32(-1.0), jnp.float32(1.0))


def hash_into(out_ref, salted_ref, lanes_ref, step):
    def hash_rows(i, carry):
        part = pl.ds(pl.multiple_of(i * step, step), step)
        out_ref[part, :] = signs_of(salted_ref[part, :], lanes_ref[...]).astype(out_ref.dtype)
        return carry

    lax.fori_loop(0, out_ref.shape[0] // step, hash_rows, 0)


def ring_index(place, count):
    upper = lax.div(place, count // 2)
    return 2 * place + upper * (2 * (count - 1 - place) + 1 - 2 * place)


def prepare_kernel(
    sizes, dy_ref, x_ref, ids_ref, col_ref, col_lanes_ref, row_ref, row_lanes_ref, moment_ref,
    all_dy_ref, all_x_ref, all_ids_ref, signs_ref, precond_ref, row_signs_ref,
    own_sem, ring_send, ring_recv, cross_send, cross_recv, x_send, x_recv, ids_send, ids_recv,
):
    groups, wide, narrow = sizes
    cols = all_dy_ref.shape[3]
    step = pl.program_id(0)
    steps = cols // signs_ref.shape[0]
    g, w, n = lax.axis_index("groups"), lax.axis_index("wide"), lax.axis_index("narrow")
    half = lax.div(w, 2)
    place = half + lax.rem(w, 2) * (wide - 1 - 2 * half)
    right = ring_index(lax.rem(place + 1, wide), wide)
    left = ring_index(lax.rem(place + wide - 1, wide), wide)
    share = wide // narrow

    def own_copies():
        slots = pl.ds(n * share, share)
        return [
            pltpu.make_async_copy(dy_ref.at[:, pl.ds(pl.multiple_of(g * cols, 128), cols)], all_dy_ref.at[w, 0], own_sem.at[0]),
            pltpu.make_async_copy(x_ref, all_x_ref.at[slots, 0], own_sem.at[1]),
            pltpu.make_async_copy(ids_ref, all_ids_ref.at[0], own_sem.at[2]),
        ]

    def cross_copies():
        made = []
        for e in range(1, groups):
            target = lax.rem(g + e, groups)
            made.append(pltpu.make_async_remote_copy(
                src_ref=dy_ref.at[:, pl.ds(pl.multiple_of(target * cols, 128), cols)], dst_ref=all_dy_ref.at[w, e],
                send_sem=cross_send.at[e], recv_sem=cross_recv.at[e], device_id=(target, w, n), device_id_type=MESH))
        return made

    def small_copies():
        made = []
        slots = pl.ds(n * share, share)
        for e in range(groups):
            target = lax.rem(g + e, groups)
            for m in range(narrow):
                if e == 0 and m == 0:
                    continue
                made.append(pltpu.make_async_remote_copy(
                    src_ref=x_ref, dst_ref=all_x_ref.at[slots, e], send_sem=x_send.at[e, m], recv_sem=x_recv.at[e, m],
                    device_id=(target, w, lax.rem(n + m, narrow)), device_id_type=MESH))
            if e > 0:
                made.append(pltpu.make_async_remote_copy(
                    src_ref=ids_ref, dst_ref=all_ids_ref.at[e], send_sem=ids_send.at[e], recv_sem=ids_recv.at[e],
                    device_id=(target, w, n), device_id_type=MESH))
        return made

    def ring_copy(e, k):
        back = lax.rem(place + (wide - k if e % 2 == 0 else k), wide)
        origin = ring_index(back, wide)
        return pltpu.make_async_remote_copy(
            src_ref=all_dy_ref.at[origin, e], dst_ref=all_dy_ref.at[origin, e],
            send_sem=ring_send.at[e, k], recv_sem=ring_recv.at[e, k],
            device_id=(g, right if e % 2 == 0 else left, n), device_id_type=MESH)

    @pl.when(step == 0)
    def _():
        barrier = pltpu.get_barrier_semaphore()
        for to in (left, right):
            pl.semaphore_signal(barrier, inc=1, device_id=(g, to, n), device_id_type=MESH)
        for e in range(groups):
            for m in range(narrow):
                if e > 0 or m > 0:
                    pl.semaphore_signal(
                        barrier, inc=1, device_id=(lax.rem(g + e, groups), w, lax.rem(n + m, narrow)), device_id_type=MESH)
        pl.semaphore_wait(barrier, 1 + groups * narrow)
        for copy in cross_copies() + own_copies() + small_copies():
            copy.start()
        own_copies()[0].wait()

    last = steps - 1
    for t in range(wide + 1):

        @pl.when(step == (min(3 * t, steps - 1) if t < wide else steps - 1))
        def _(t=t):
            if t == 1:
                for copy in cross_copies():
                    copy.wait_recv()
            for e in range(groups):
                k = t - (e > 0)
                if 1 <= k <= wide - 1:
                    ring_copy(e, k - 1).wait_recv()
                if 0 <= k <= wide - 2:
                    ring_copy(e, k).start()

    @pl.when(step == 1)
    def _():
        hash_into(row_signs_ref, row_ref, row_lanes_ref, 32)

    hash_into(signs_ref, col_ref, col_lanes_ref, 64)

    def moment_rows(i, carry):
        rows = pl.ds(pl.multiple_of(i * 32, 32), 32)
        precond_ref[rows, :] = 1.0 / (jnp.sqrt(moment_ref[rows, :]) + adam_epsilon)
        return carry

    lax.fori_loop(0, moment_ref.shape[0] // 32, moment_rows, 0)

    @pl.when(step == last)
    def _():
        for copy in own_copies()[1:]:
            copy.wait()
        for copy in cross_copies():
            copy.wait_send()
        for copy in small_copies():
            copy.wait()
        for e in range(groups):
            for k in range(wide - 1):
                ring_copy(e, k).wait_send()


def map_kernel(x_ref, which_ref, dy_ref, precond_ref, signs_ref, rows_ref, out_ref, picked_ref):
    @pl.when(pl.program_id(0) == 0)
    def _():
        out_ref[...] = jnp.zeros_like(out_ref)
        turned = x_ref[...].T
        for s in range(picked_ref.shape[0]):
            picked_ref[s] = jnp.where(which_ref[...] == s, turned.astype(jnp.float32), 0.0).astype(jnp.bfloat16)

    for s in range(picked_ref.shape[0]):
        grad = jnp.dot(picked_ref[s], dy_ref[...], preferred_element_type=jnp.float32)
        scaled = (grad * precond_ref[...]).astype(jnp.bfloat16)
        mapped = jnp.dot(scaled, signs_ref[...], preferred_element_type=jnp.float32)
        out_ref[s : s + 1, :] += jnp.sum(mapped * rows_ref[...], axis=0, keepdims=True)


def reduce_kernel(sizes, terms_ref, out_ref, near, mine, far, near_send, near_recv, far_send, far_recv):
    groups, wide, narrow = sizes
    g, w, n = lax.axis_index("groups"), lax.axis_index("wide"), lax.axis_index("narrow")

    def near_copy(e, m):
        return pltpu.make_async_remote_copy(
            src_ref=terms_ref.at[e], dst_ref=near.at[e * narrow + m],
            send_sem=near_send.at[e * narrow + m], recv_sem=near_recv.at[e * narrow + m],
            device_id=(lax.rem(g + groups - e, groups), w, lax.rem(n + m, narrow)), device_id_type=MESH)

    def far_copy(v):
        return pltpu.make_async_remote_copy(
            src_ref=mine, dst_ref=far.at[v], send_sem=far_send.at[v], recv_sem=far_recv.at[v],
            device_id=(g, lax.rem(w + v, wide), n), device_id_type=MESH)

    near_list = [(e, m) for e in range(groups) for m in range(narrow) if e > 0 or m > 0]
    barrier = pltpu.get_barrier_semaphore()
    for e, m in near_list:
        pl.semaphore_signal(
            barrier, inc=1, device_id=(lax.rem(g + e, groups), w, lax.rem(n + m, narrow)), device_id_type=MESH)
    for v in range(1, wide):
        pl.semaphore_signal(barrier, inc=1, device_id=(g, lax.rem(w + v, wide), n), device_id_type=MESH)
    pl.semaphore_wait(barrier, len(near_list) + wide - 1)

    for e, m in near_list:
        near_copy(e, m).start()
    total = terms_ref[0]
    for e, m in near_list:
        near_copy(e, m).wait_recv()
        total = total + near[e * narrow + m]
    mine[...] = total
    for v in range(1, wide):
        far_copy(v).start()
    for v in range(1, wide):
        far_copy(v).wait_recv()
        total = total + far[v]
    out_ref[...] = total * (1.0 / (float(D) * float(FF)) ** 0.5)
    for e, m in near_list:
        near_copy(e, m).wait_send()
    for v in range(1, wide):
        far_copy(v).wait_send()


def on_device(activations, out_grads, second_moment, seq_ids, seed_word, row_keys, col_keys):
    sizes = groups, wide, narrow = tuple(lax.axis_size(name) for name in ("groups", "wide", "narrow"))
    me = lax.axis_index("groups")
    rows, all_cols = second_moment.shape
    cols = all_cols // groups
    tokens = seq_ids.shape[0]
    per = out_grads.shape[0]
    chunk = 1280 if cols % 1280 == 0 else 640
    small = 256 if cols % 256 == 0 else 128
    steps = cols // small

    seed = seed_word[0]
    lane = jnp.arange(K, dtype=jnp.int32)[None, :]
    row_salted = scramble(row_keys ^ (seed + 1))[:, None]
    my_keys = lax.dynamic_slice_in_dim(col_keys, me * cols, cols)
    col_salted = scramble(my_keys ^ (seed + 2))[:, None]
    row_lanes = scramble(lane + 1)
    col_lanes = scramble(lane + 2)

    any_space = pl.BlockSpec(memory_space=pl.ANY)
    dma = pltpu.SemaphoreType.DMA
    all_dy, all_x, all_ids, signs, precond, row_signs = pl.pallas_call(
        functools.partial(prepare_kernel, sizes),
        grid=(steps,),
        in_specs=[
            any_space,
            any_space,
            any_space,
            pl.BlockSpec((small, 1), lambda i: (i, 0)),
            pl.BlockSpec((1, K), lambda i: (0, 0)),
            pl.BlockSpec((rows, 1), lambda i: (0, 0)),
            pl.BlockSpec((1, K), lambda i: (0, 0)),
            pl.BlockSpec((rows, small), lambda i: (0, lax.axis_index("groups") * steps + i)),
        ],
        out_specs=[
            any_space,
            any_space,
            any_space,
            pl.BlockSpec((small, K), lambda i: (i, 0)),
            pl.BlockSpec((rows, small), lambda i: (0, i)),
            pl.BlockSpec((rows, K), lambda i: (0, 0)),
        ],
        out_shape=[
            jax.ShapeDtypeStruct((wide, groups, per, cols), jnp.bfloat16),
            jax.ShapeDtypeStruct((wide, groups, per, rows), jnp.bfloat16),
            jax.ShapeDtypeStruct((groups, 1, tokens), jnp.int32),
            jax.ShapeDtypeStruct((cols, K), jnp.bfloat16),
            jax.ShapeDtypeStruct((rows, cols), jnp.float32),
            jax.ShapeDtypeStruct((rows, K), jnp.float32),
        ],
        scratch_shapes=[
            dma((3,)),
            dma((groups, wide)),
            dma((groups, wide)),
            dma((groups,)),
            dma((groups,)),
            dma((groups, narrow)),
            dma((groups, narrow)),
            dma((groups,)),
            dma((groups,)),
        ],
        compiler_params=pltpu.CompilerParams(vmem_limit_bytes=40 << 20, collective_id=0, has_side_effects=True),
        cost_estimate=pl.CostEstimate(flops=cols * K * 20, bytes_accessed=rows * cols * 8 + cols * K * 2, transcendentals=2 * rows * cols),
        name="prepare",
    )(
        out_grads, activations.reshape(wide // narrow, per, rows), seq_ids.reshape(1, tokens),
        col_salted, col_lanes, row_salted, row_lanes, second_moment,
    )

    count = groups * tokens
    which = all_ids.reshape(groups, wide, per) + SEQS * jnp.arange(groups, dtype=jnp.int32)[:, None, None]
    which = which.transpose(1, 0, 2).reshape(1, count)

    terms = pl.pallas_call(
        map_kernel,
        grid=(cols // chunk,),
        in_specs=[
            pl.BlockSpec((count, rows), lambda i: (0, 0)),
            pl.BlockSpec((1, count), lambda i: (0, 0)),
            pl.BlockSpec((count, chunk), lambda i: (0, i)),
            pl.BlockSpec((rows, chunk), lambda i: (0, i)),
            pl.BlockSpec((chunk, K), lambda i: (i, 0)),
            pl.BlockSpec((rows, K), lambda i: (0, 0)),
        ],
        out_specs=pl.BlockSpec((groups * SEQS, K), lambda i: (0, 0)),
        out_shape=jax.ShapeDtypeStruct((groups * SEQS, K), jnp.float32),
        scratch_shapes=[pltpu.VMEM((groups * SEQS, rows, count), jnp.bfloat16)],
        compiler_params=pltpu.CompilerParams(vmem_limit_bytes=58 << 20),
        cost_estimate=pl.CostEstimate(
            flops=2 * groups * SEQS * rows * cols * (K + 256), bytes_accessed=cols * (rows * 4 + K * 2), transcendentals=0),
        name="map",
    )(all_x.reshape(count, rows), which, all_dy.reshape(count, cols), precond, signs, row_signs)

    close = groups * narrow
    return pl.pallas_call(
        functools.partial(reduce_kernel, sizes),
        in_specs=[pl.BlockSpec(memory_space=pltpu.VMEM)],
        out_specs=pl.BlockSpec(memory_space=pltpu.VMEM),
        out_shape=jax.ShapeDtypeStruct((SEQS, K), jnp.float32),
        scratch_shapes=[
            pltpu.VMEM((close, SEQS, K), jnp.float32),
            pltpu.VMEM((SEQS, K), jnp.float32),
            pltpu.VMEM((wide, SEQS, K), jnp.float32),
            dma((close,)),
            dma((close,)),
            dma((wide,)),
            dma((wide,)),
        ],
        compiler_params=pltpu.CompilerParams(collective_id=1, has_side_effects=True),
        name="reduce",
    )(terms.reshape(groups, SEQS, K))


def solution(mesh):
    placed = (
        P(("groups", "narrow"), "wide"),
        P(("groups", "wide"), "narrow"),
        P("wide", "narrow"),
        P("groups"),
        P(),
        P("wide"),
        P("narrow"),
    )
    return jax.shard_map(
        on_device, mesh=mesh, in_specs=placed, out_specs=P("groups", None), check_vma=False
    )
```

time: 232 us -> 131 us (0.56)
  matrix products: 127 us -> 0 us
  Pallas kernels: 0 us -> 115 us
  waiting for transfers between devices: 59.8 us -> 0 us
  blocking collectives: 24.5 us -> 0 us
  between operations: 14.1 us -> 0.73 us
  local copies, waits for them, and re-layouts: 0.01 us -> 11.3 us
  other arithmetic: 6.14 us -> 2.33 us
    dot_general x3 -> x0, matrix products: 127 us -> none  [the longest x1 81.5 us: on_device(): jnp.dot(stacked, col_signs, preferred_element_type=jnp.float32)]
    pallas_call x0 -> x3, Pallas kernels: none -> 115 us  [the longest x1 55.2 us: on_device(): pl.pallas_call(functools.partial(prepare_kernel, sizes), grid=(steps,), i...]
    all_gather x1 -> x0, waiting for transfers between devices: 59.1 us -> none  [on_device(): whole_dy = lax.all_gather(out_grads, 'wide', axis=0, tiled=True)]
    psum x2 -> x0, blocking collectives: 22.3 us -> none  [the longest x1 19.8 us: on_device(): features = lax.psum(paired, 'wide')]
    unnamed x4 -> x13, local copies, waits for them, and re-layouts: 0.01 us -> 7.69 us
    convert_element_type x1 -> x0, other arithmetic: 2.84 us -> none  [rademacher(): return (1 - 2 * parity).astype(jnp.float32)]
  transfers between devices with their start and end apart: 1 -> 0, of which waited for: 1 -> 0; matrix products, arithmetic and copies ran while one was open for 2% -> 0% of each run, Pallas kernels for 0% -> 0%
where the time goes in v2:
time: 131 us; the launch traced here: 130 us
  Pallas kernels  115 us (88%)
  local copies, waits for them, and re-layouts  11.3 us (9%)
  other arithmetic  2.33 us (2%)
    pallas_call x1, Pallas kernels, on_device(): pl.pallas_call(functools.partial(prepare_kernel, sizes), grid=(steps,), i...  55.2 us
    pallas_call x1, Pallas kernels, on_device(): pl.pallas_call(map_kernel, grid=(cols // chunk,), in_specs=[pl.BlockSpec(...  48.9 us
    pallas_call x1, Pallas kernels, on_device(): pl.pallas_call(functools.partial(reduce_kernel, sizes), in_specs=[pl.Bloc...  11.2 us
    unnamed x13, local copies, waits for them, and re-layouts  7.69 us

profile of v2, /device:TPU:0, one launch (start us, length us, event | category | flops | bytes accessed | tf_op | source)
XLA Modules:
  0.0 129.7 jit_solution(192300801757021919)
XLA Ops:
  0.7 0.9 shift-right-logical_xor_fusion
  1.5 0.9 broadcast_in_dim.34.col_ref
  2.4 0.7 shift-right-logical_xor_fusion.6
  3.1 0.1 broadcast_in_dim.35.row_ref
  3.3 0.0 copy-start
  3.3 1.0 copy-done
  4.3 0.0 copy-start.1
  4.3 0.9 copy-done.1
  5.2 0.0 copy-start.2
  5.2 0.7 copy-done.2
  5.9 55.2 %prepare.1 = (bf16[8,2,16,6400]{3,2,1,0:T(8,128)(2,1)S(1)}, bf16[8,2,16,640]{3,2,1,0:T(8,128)(2,1)S(1)}, s32[2,1,128]{2,1,0:T(1,128)S(1)}, bf16[6400,1024]{1,0:T...) custom-call(bf16[16,12800]{1,0:T(8,128)(2,1)S(1)} %copy-done, bf16[4,16,640]{2,1,0:T(8,128)(2,1)S(1)} %bitcast.8, ...), custom_call_target="tpu_custom_call" | custom-call | flops 131072000 | bytes 45875200 | tf_op jit(solution)/shard_map/prepare/pallas_call | solution.py:246
  61.1 0.0 copy-start.3
  61.1 1.7 %copy-done.3 = bf16[8,2,16,6400]{3,2,1,0:T(8,128)(2,1)} copy-done((bf16[8,2,16,6400]{3,2,1,0:T(8,128)(2,1)}, bf16[8,2,16,6400]{3,2,1,0:T(8,128)(2,1)S(1)}, u32[]{:S(2)}) %copy-start.3) | copy-done | bytes 3276824
  62.8 0.0 copy-start.4
  62.8 1.5 %copy-done.4 = f32[640,1024]{1,0:T(8,128)} copy-done((f32[640,1024]{1,0:T(8,128)}, f32[640,1024]{1,0:T(8,128)S(1)}, u32[]{:S(2)}) %copy-start.4) | copy-done | bytes 2621464
  64.2 0.0 copy-start.5
  64.2 0.7 copy-done.5
  64.9 0.5 broadcast.161
  65.4 0.7 reduce.4
  66.1 0.1 reshape.121
  66.2 0.1 add_bitcast_fusion
  66.3 0.7 reshape.122.which_ref
  66.9 48.9 %map.1 = f32[4,1024]{1,0:T(4,128)} custom-call(bf16[256,640]{1,0:T(8,128)(2,1)} %bitcast.11, s32[1,256]{1,0:T(1,128)} %reshape.122.which_ref, bf16[256,6400]{1,0:T(8,128)(2,1)} %bitcast.10, f32[640,6400]{1,0:T(8,128)} %get-tuple-element.14.precond_ref, bf16[6400,1024]{1,0:T(8,128)(2,1)} %get-tuple-element.15.signs_ref, f32[640,1024]{1,0:T(8,128)} %copy-done.4), custom_call_target="tpu_custom_call" | custom-call | flops 41943040000 | bytes 29491200 | tf_op jit(solution)/shard_map/map/pallas_call | solution.py:298
  115.8 1.3 %reshape.124.terms_ref = f32[2,2,1024]{2,1,0:T(2,128)} reshape(f32[4,1024]{1,0:T(4,128)} %map.1) | data formatting | bytes 32768 | tf_op jit(solution)/shard_map/reshape | solution.py:335
  117.2 11.2 %reduce.5 = f32[2,1024]{1,0:T(2,128)} custom-call(f32[2,2,1024]{2,1,0:T(2,128)} %reshape.124.terms_ref), custom_call_target="tpu_custom_call" | custom-call | tf_op jit(solution)/shard_map/reduce/pallas_call | solution.py:319
  128.4 1.3 copy.17
  (3 shorter events, 0.0 us)
Async XLA Ops:
  3.3 1.0 copy-start
  4.3 0.9 copy-start.1
  5.2 0.7 copy-start.2
  61.1 1.7 %copy-start.3 = (bf16[8,2,16,6400]{3,2,1,0:T(8,128)(2,1)}, bf16[8,2,16,6400]{3,2,1,0:T(8,128)(2,1)S(1)}, u32[]{:S(2)}) copy-start(bf16[8,2,16,6400]{3,2,1,0:T(8,128)(2,1)S(1)} %get-tuple-element.13) | copy-start | bytes 9830404
  62.8 1.5 %copy-start.4 = (f32[640,1024]{1,0:T(8,128)}, f32[640,1024]{1,0:T(8,128)S(1)}, u32[]{:S(2)}) copy-start(f32[640,1024]{1,0:T(8,128)S(1)} %get-tuple-element.16.rows_ref) | copy-start | bytes 7864324
  64.2 0.7 copy-start.5

commit v3 on v2

--- a/solution.py
+++ b/solution.py
@@ -50,38 +50,103 @@
     return 2 * place + upper * (2 * (count - 1 - place) + 1 - 2 * place)
 
 
+class Ring:
+    def __init__(self, sizes, dy_ref, into_ref, sems, base, cols):
+        self.sizes, self.dy_ref, self.into_ref = sizes, dy_ref, into_ref
+        self.own_sem, self.send, self.recv, self.cross_send, self.cross_recv = sems
+        self.base, self.cols, self.width = base, cols, into_ref.shape[3]
+        wide = sizes[1]
+        self.g, self.w, self.n = lax.axis_index("groups"), lax.axis_index("wide"), lax.axis_index("narrow")
+        half = lax.div(self.w, 2)
+        self.place = half + lax.rem(self.w, 2) * (wide - 1 - 2 * half)
+        self.right = ring_index(lax.rem(self.place + 1, wide), wide)
+        self.left = ring_index(lax.rem(self.place + wide - 1, wide), wide)
+
+    def block(self, group):
+        start = pl.multiple_of(group * self.cols + self.base, 128)
+        return self.dy_ref.at[:, pl.ds(start, self.width)]
+
+    def own(self):
+        return pltpu.make_async_copy(self.block(self.g), self.into_ref.at[self.w, 0], self.own_sem.at[0])
+
+    def cross(self):
+        made = []
+        for e in range(1, self.sizes[0]):
+            target = lax.rem(self.g + e, self.sizes[0])
+            made.append(pltpu.make_async_remote_copy(
+                src_ref=self.block(target), dst_ref=self.into_ref.at[self.w, e],
+                send_sem=self.cross_send.at[e], recv_sem=self.cross_recv.at[e],
+                device_id=(target, self.w, self.n), device_id_type=MESH))
+        return made
+
+    def hop(self, e, k):
+        wide = self.sizes[1]
+        origin = ring_index(lax.rem(self.place + (wide - k if e % 2 == 0 else k), wide), wide)
+        return pltpu.make_async_remote_copy(
+            src_ref=self.into_ref.at[origin, e], dst_ref=self.into_ref.at[origin, e],
+            send_sem=self.send.at[e, k], recv_sem=self.recv.at[e, k],
+            device_id=(self.g, self.right if e % 2 == 0 else self.left, self.n), device_id_type=MESH)
+
+    def stage(self, t):
+        groups, wide, _ = self.sizes
+        if t == 0:
+            for copy in self.cross() + [self.own()]:
+                copy.start()
+            self.own().wait()
+        if t == 1:
+            for copy in self.cross():
+                copy.wait_recv()
+        for e in range(groups):
+            k = t - (e > 0)
+            if 1 <= k <= wide - 1:
+                self.hop(e, k - 1).wait_recv()
+            if 0 <= k <= wide - 2:
+                self.hop(e, k).start()
+
+    def finish(self):
+        for copy in self.cross():
+            copy.wait_send()
+        for e in range(self.sizes[0]):
+            for k in range(self.sizes[1] - 1):
+                self.hop(e, k).wait_send()
+
+
+def ring_semaphores(sizes):
+    dma = pltpu.SemaphoreType.DMA
+    return [dma((1,)), dma(sizes[:2]), dma(sizes[:2]), dma(sizes[:1]), dma(sizes[:1])]
+
+
+def greet(sizes, left, right, cores):
+    groups, _, narrow = sizes
+    g, w, n = lax.axis_index("groups"), lax.axis_index("wide"), lax.axis_index("narrow")
+    barrier = pltpu.get_barrier_semaphore()
+    for to in (left, right):
+        pl.semaphore_signal(barrier, inc=1, device_id=(g, to, n), device_id_type=MESH)
+    for e in range(groups):
+        for m in range(cores):
+            if e > 0 or m > 0:
+                pl.semaphore_signal(
+                    barrier, inc=1, device_id=(lax.rem(g + e, groups), w, lax.rem(n + m, narrow)), device_id_type=MESH)
+    pl.semaphore_wait(barrier, 1 + groups * cores)
+
+
 def prepare_kernel(
-    sizes, dy_ref, x_ref, ids_ref, col_ref, col_lanes_ref, row_ref, row_lanes_ref, moment_ref,
+    sizes, cols, dy_ref, x_ref, ids_ref, col_ref, col_lanes_ref, row_ref, row_lanes_ref, moment_ref,
     all_dy_ref, all_x_ref, all_ids_ref, signs_ref, precond_ref, row_signs_ref,
-    own_sem, ring_send, ring_recv, cross_send, cross_recv, x_send, x_recv, ids_send, ids_recv,
+    small_sem, x_send, x_recv, ids_send, ids_recv, *ring_sems,
 ):
     groups, wide, narrow = sizes
-    cols = all_dy_ref.shape[3]
     step = pl.program_id(0)
     steps = cols // signs_ref.shape[0]
     g, w, n = lax.axis_index("groups"), lax.axis_index("wide"), lax.axis_index("narrow")
-    half = lax.div(w, 2)
-    place = half + lax.rem(w, 2) * (wide - 1 - 2 * half)
-    right = ring_index(lax.rem(place + 1, wide), wide)
-    left = ring_index(lax.rem(place + wide - 1, wide), wide)
     share = wide // narrow
+    ring = Ring(sizes, dy_ref, all_dy_ref, ring_sems, 0, cols)
 
     def own_copies():
-        slots = pl.ds(n * share, share)
         return [
-            pltpu.make_async_copy(dy_ref.at[:, pl.ds(pl.multiple_of(g * cols, 128), cols)], all_dy_ref.at[w, 0], own_sem.at[0]),
-            pltpu.make_async_copy(x_ref, all_x_ref.at[slots, 0], own_sem.at[1]),
-            pltpu.make_async_copy(ids_ref, all_ids_ref.at[0], own_sem.at[2]),
+            pltpu.make_async_copy(x_ref, all_x_ref.at[pl.ds(n * share, share), 0], small_sem.at[0]),
+            pltpu.make_async_copy(ids_ref, all_ids_ref.at[0], small_sem.at[1]),
         ]
-
-    def cross_copies():
-        made = []
-        for e in range(1, groups):
-            target = lax.rem(g + e, groups)
-            made.append(pltpu.make_async_remote_copy(
-                src_ref=dy_ref.at[:, pl.ds(pl.multiple_of(target * cols, 128), cols)], dst_ref=all_dy_ref.at[w, e],
-                send_sem=cross_send.at[e], recv_sem=cross_recv.at[e], device_id=(target, w, n), device_id_type=MESH))
-        return made
 
     def small_copies():
         made = []
@@ -100,43 +165,21 @@
                     device_id=(target, w, n), device_id_type=MESH))
         return made
 
-    def ring_copy(e, k):
-        back = lax.rem(place + (wide - k if e % 2 == 0 else k), wide)
-        origin = ring_index(back, wide)
-        return pltpu.make_async_remote_copy(
-            src_ref=all_dy_ref.at[origin, e], dst_ref=all_dy_ref.at[origin, e],
-            send_sem=ring_send.at[e, k], recv_sem=ring_recv.at[e, k],
-            device_id=(g, right if e % 2 == 0 else left, n), device_id_type=MESH)
-
     @pl.when(step == 0)
     def _():
-        barrier = pltpu.get_barrier_semaphore()
-        for to in (left, right):
-            pl.semaphore_signal(barrier, inc=1, device_id=(g, to, n), device_id_type=MESH)
-        for e in range(groups):
-            for m in range(narrow):
-                if e > 0 or m > 0:
-                    pl.semaphore_signal(
-                        barrier, inc=1, device_id=(lax.rem(g + e, groups), w, lax.rem(n + m, narrow)), device_id_type=MESH)
-        pl.semaphore_wait(barrier, 1 + groups * narrow)
-        for copy in cross_copies() + own_copies() + small_copies():
-            copy.start()
-        own_copies()[0].wait()
+        greet(sizes, ring.left, ring.right, narrow)
 
     last = steps - 1
     for t in range(wide + 1):
 
-        @pl.when(step == (min(3 * t, steps - 1) if t < wide else steps - 1))
+        @pl.when(step == (min(3 * t, last) if t < wide else last))
         def _(t=t):
-            if t == 1:
-                for copy in cross_copies():
-                    copy.wait_recv()
-            for e in range(groups):
-                k = t - (e > 0)
-                if 1 <= k <= wide - 1:
-                    ring_copy(e, k - 1).wait_recv()
-                if 0 <= k <= wide - 2:
-                    ring_copy(e, k).start()
+            ring.stage(t)
+
+    @pl.when(step == 0)
+    def _():
+        for copy in own_copies() + small_copies():
+            copy.start()
 
     @pl.when(step == 1)
     def _():
@@ -153,30 +196,60 @@
 
     @pl.when(step == last)
     def _():
-        for copy in own_copies()[1:]:
+        for copy in own_copies() + small_copies():
             copy.wait()
-        for copy in cross_copies():
-            copy.wait_send()
-        for copy in small_copies():
-            copy.wait()
-        for e in range(groups):
-            for k in range(wide - 1):
-                ring_copy(e, k).wait_send()
-
-
-def map_kernel(x_ref, which_ref, dy_ref, precond_ref, signs_ref, rows_ref, out_ref, picked_ref):
-    @pl.when(pl.program_id(0) == 0)
-    def _():
+        ring.finish()
+
+
+def map_kernel(
+    sizes, cols, early, x_ref, which_ref, early_dy_ref, dy_ref, precond_ref, signs_ref, rows_ref,
+    out_ref, picked_ref, late_ref, now_ref, *ring_sems,
+):
+    groups, wide, _ = sizes
+    i = pl.program_id(0)
+    count, chunk = now_ref.shape
+    many = picked_ref.shape[0]
+    chunks = cols // chunk
+    ring = Ring(sizes, dy_ref, late_ref, ring_sems, early * chunk, cols)
+    stages = wide + 1
+    slots = early * many
+
+    @pl.when(i == 0)
+    def _():
+        greet(sizes, ring.left, ring.right, 1)
+        ring.stage(0)
         out_ref[...] = jnp.zeros_like(out_ref)
-        turned = x_ref[...].T
-        for s in range(picked_ref.shape[0]):
-            picked_ref[s] = jnp.where(which_ref[...] == s, turned.astype(jnp.float32), 0.0).astype(jnp.bfloat16)
-
-    for s in range(picked_ref.shape[0]):
-        grad = jnp.dot(picked_ref[s], dy_ref[...], preferred_element_type=jnp.float32)
+        turned = x_ref[...].T.astype(jnp.float32)
+        for s in range(many):
+            picked_ref[s] = jnp.where(which_ref[...] == s, turned, 0.0).astype(jnp.bfloat16)
+
+    @pl.when(i < early)
+    def _():
+        now_ref[...] = early_dy_ref[...]
+
+    for c in range(early, chunks):
+
+        @pl.when(i == c)
+        def _(c=c):
+            now_ref[...] = late_ref[:, :, :, (c - early) * chunk : (c - early + 1) * chunk].reshape(count, chunk)
+
+    for s in range(many):
+        for t in range(1, stages):
+            slot = t if stages <= slots else t * slots // stages
+            if slot % many == s:
+
+                @pl.when(i == slot // many)
+                def _(t=t):
+                    ring.stage(t)
+
+        grad = jnp.dot(picked_ref[s], now_ref[...], preferred_element_type=jnp.float32)
         scaled = (grad * precond_ref[...]).astype(jnp.bfloat16)
         mapped = jnp.dot(scaled, signs_ref[...], preferred_element_type=jnp.float32)
-        out_ref[s : s + 1, :] += jnp.sum(mapped * rows_ref[...], axis=0, keepdims=True)
+        out_ref[s // SEQS, s % SEQS : s % SEQS + 1, :] += jnp.sum(mapped * rows_ref[...], axis=0, keepdims=True)
+
+    @pl.when(i == chunks - 1)
+    def _():
+        ring.finish()
 
 
 def reduce_kernel(sizes, terms_ref, out_ref, near, mine, far, near_send, near_recv, far_send, far_recv):
@@ -232,6 +305,8 @@
     chunk = 1280 if cols % 1280 == 0 else 640
     small = 256 if cols % 256 == 0 else 128
     steps = cols // small
+    chunks = cols // chunk
+    early = chunks - 2
 
     seed = seed_word[0]
     lane = jnp.arange(K, dtype=jnp.int32)[None, :]
@@ -244,7 +319,7 @@
     any_space = pl.BlockSpec(memory_space=pl.ANY)
     dma = pltpu.SemaphoreType.DMA
     all_dy, all_x, all_ids, signs, precond, row_signs = pl.pallas_call(
-        functools.partial(prepare_kernel, sizes),
+        functools.partial(prepare_kernel, sizes, cols),
         grid=(steps,),
         in_specs=[
             any_space,
@@ -265,7 +340,7 @@
             pl.BlockSpec((rows, K), lambda i: (0, 0)),
         ],
         out_shape=[
-            jax.ShapeDtypeStruct((wide, groups, per, cols), jnp.bfloat16),
+            jax.ShapeDtypeStruct((wide, groups, per, early * chunk), jnp.bfloat16),
             jax.ShapeDtypeStruct((wide, groups, per, rows), jnp.bfloat16),
             jax.ShapeDtypeStruct((groups, 1, tokens), jnp.int32),
             jax.ShapeDtypeStruct((cols, K), jnp.bfloat16),
@@ -273,17 +348,10 @@
             jax.ShapeDtypeStruct((rows, K), jnp.float32),
         ],
         scratch_shapes=[
-            dma((3,)),
-            dma((groups, wide)),
-            dma((groups, wide)),
-            dma((groups,)),
-            dma((groups,)),
-            dma((groups, narrow)),
-            dma((groups, narrow)),
-            dma((groups,)),
-            dma((groups,)),
-        ],
-        compiler_params=pltpu.CompilerParams(vmem_limit_bytes=40 << 20, collective_id=0, has_side_effects=True),
+            dma((2,)), dma((groups, narrow)), dma((groups, narrow)), dma((groups,)), dma((groups,)),
+            *ring_semaphores(sizes),
+        ],
+        compiler_params=pltpu.CompilerParams(vmem_limit_bytes=60 << 20, collective_id=0, has_side_effects=True),
         cost_estimate=pl.CostEstimate(flops=cols * K * 20, bytes_accessed=rows * cols * 8 + cols * K * 2, transcendentals=2 * rows * cols),
         name="prepare",
     )(
@@ -296,24 +364,30 @@
     which = which.transpose(1, 0, 2).reshape(1, count)
 
     terms = pl.pallas_call(
-        map_kernel,
+        functools.partial(map_kernel, sizes, cols, early),
         grid=(cols // chunk,),
         in_specs=[
             pl.BlockSpec((count, rows), lambda i: (0, 0)),
             pl.BlockSpec((1, count), lambda i: (0, 0)),
-            pl.BlockSpec((count, chunk), lambda i: (0, i)),
+            pl.BlockSpec((count, chunk), lambda i: (0, jnp.minimum(i, early - 1))),
+            any_space,
             pl.BlockSpec((rows, chunk), lambda i: (0, i)),
             pl.BlockSpec((chunk, K), lambda i: (i, 0)),
             pl.BlockSpec((rows, K), lambda i: (0, 0)),
         ],
-        out_specs=pl.BlockSpec((groups * SEQS, K), lambda i: (0, 0)),
-        out_shape=jax.ShapeDtypeStruct((groups * SEQS, K), jnp.float32),
-        scratch_shapes=[pltpu.VMEM((groups * SEQS, rows, count), jnp.bfloat16)],
-        compiler_params=pltpu.CompilerParams(vmem_limit_bytes=58 << 20),
+        out_specs=pl.BlockSpec((groups, SEQS, K), lambda i: (0, 0, 0)),
+        out_shape=jax.ShapeDtypeStruct((groups, SEQS, K), jnp.float32),
+        scratch_shapes=[
+            pltpu.VMEM((groups * SEQS, rows, count), jnp.bfloat16),
+            pltpu.VMEM((wide, groups, per, (chunks - early) * chunk), jnp.bfloat16),
+            pltpu.VMEM((count, chunk), jnp.bfloat16),
+            *ring_semaphores(sizes),
+        ],
+        compiler_params=pltpu.CompilerParams(vmem_limit_bytes=60 << 20, collective_id=2, has_side_effects=True),
         cost_estimate=pl.CostEstimate(
             flops=2 * groups * SEQS * rows * cols * (K + 256), bytes_accessed=cols * (rows * 4 + K * 2), transcendentals=0),
         name="map",
-    )(all_x.reshape(count, rows), which, all_dy.reshape(count, cols), precond, signs, row_signs)
+    )(all_x.reshape(count, rows), which, all_dy.reshape(count, early * chunk), out_grads, precond, signs, row_signs)
 
     close = groups * narrow
     return pl.pallas_call(
@@ -332,7 +406,7 @@
         ],
         compiler_params=pltpu.CompilerParams(collective_id=1, has_side_effects=True),
         name="reduce",
-    )(terms.reshape(groups, SEQS, K))
+    )(terms)
 
 
 def solution(mesh):

time: 131 us -> 142 us (1.084)
  Pallas kernels: 115 us -> 129 us
  local copies, waits for them, and re-layouts: 11.3 us -> 7.72 us
    pallas_call x2, Pallas kernels: 104 us -> 119 us  [the longest x1 66.3 us: on_device(): pl.pallas_call(functools.partial(map_kernel, sizes, cols, early), grid=(c...]
    unnamed x13 -> x1, local copies, waits for them, and re-layouts: 7.69 us -> 1.3 us
    broadcast_in_dim x1, local copies, waits for them, and re-layouts: 0.9 us -> 4.27 us  [on_device(): col_salted = scramble(my_keys ^ seed + 2)[:, None]]
where the time goes in v3:
time: 142 us; the launch traced here: 141 us
  Pallas kernels  129 us (91%)
  local copies, waits for them, and re-layouts  7.72 us (5%)
  other arithmetic  3.53 us (2%)
    pallas_call x1, Pallas kernels, on_device(): pl.pallas_call(functools.partial(map_kernel, sizes, cols, early), grid=(c...  66.3 us
    pallas_call x1, Pallas kernels, on_device(): pl.pallas_call(functools.partial(prepare_kernel, sizes, cols), grid=(step...  52.2 us
    pallas_call x1, Pallas kernels, on_device(): pl.pallas_call(functools.partial(reduce_kernel, sizes), in_specs=[pl.Bloc...  10.3 us
    broadcast_in_dim x1, local copies, waits for them, and re-layouts, on_device(): col_salted = scramble(my_keys ^ seed + 2)[:, None]  4.27 us

profile of v3, /device:TPU:0, one launch (start us, length us, event | category | flops | bytes accessed | tf_op | source)
XLA Modules:
  0.0 140.8 jit_solution(13198623705969875713)
XLA Ops:
  0.7 0.9 shift-right-logical_xor_fusion
  1.5 4.3 %broadcast_in_dim.34.col_ref = s32[6400,1]{1,0:T(8,128)} reshape(s32[6400]{0:T(1024)S(1)} %shift-right-logical_xor_fusion) | data formatting | bytes 51200 | tf_op jit(solution)/shard_map/broadcast_in_dim | solution.py:315
  5.8 0.7 shift-right-logical_xor_fusion.6
  6.5 0.9 broadcast_in_dim.35.row_ref
  7.4 0.6 shift-right-logical_xor_fusion.3
  8.0 52.2 %prepare.1 = (bf16[8,2,16,3840]{3,2,1,0:T(8,128)(2,1)}, bf16[8,2,16,640]{3,2,1,0:T(8,128)(2,1)}, s32[2,1,128]{2,1,0:T(1,128)}, bf16[6400,1024]{1,0:T(8,128)(2,1)...) custom-call(bf16[16,12800]{1,0:T(8,128)(2,1)} %dy_ref.3, bf16[4,16,640]{2,1,0:T(8,128)(2,1)} %bitcast.8, s32[1,128]{1,0:T(1,128)} %bitcast.9, ...), custom_call_target="tpu_custom_call" | custom-call | flops 131072000 | bytes 45875200 | tf_op jit(solution)/shard_map/prepare/pallas_call | solution.py:321
  60.2 0.5 broadcast.161
  60.7 1.3 reduce.4
  62.0 0.1 reshape.118
  62.1 0.1 add_bitcast_fusion
  62.2 0.7 reshape.119.which_ref
  62.9 66.3 %map.1.terms_ref = f32[2,2,1024]{2,1,0:T(2,128)} custom-call(bf16[256,640]{1,0:T(8,128)(2,1)} %bitcast.11, s32[1,256]{1,0:T(1,128)} %reshape.119.which_ref, bf16[256,3840]{1,0:T(8,128)(2,1)} %bitcast.10, bf16[16,12800]{1,0:T(8,128)(2,1)} %dy_ref.3, f32[640,6400]{1,0:T(8,128)} %get-tuple-element.14.precond_ref, ...), custom_call_target="tpu_custom_call" | custom-call | flops 41943040000 | bytes 29491200 | tf_op jit(solution)/shard_map/map/pallas_call | solution.py:366
  129.2 10.3 %reduce.5 = f32[2,1024]{1,0:T(2,128)} custom-call(f32[2,2,1024]{2,1,0:T(2,128)} %map.1.terms_ref), custom_call_target="tpu_custom_call" | custom-call | tf_op jit(solution)/shard_map/reduce/pallas_call | solution.py:393
  139.5 1.3 copy.17
  (2 shorter events, 0.0 us)

commit v4 on v2

--- a/solution.py
+++ b/solution.py
@@ -142,14 +142,17 @@
     def _():
         hash_into(row_signs_ref, row_ref, row_lanes_ref, 32)
 
-    hash_into(signs_ref, col_ref, col_lanes_ref, 64)
-
-    def moment_rows(i, carry):
-        rows = pl.ds(pl.multiple_of(i * 32, 32), 32)
+    turns = signs_ref.shape[0] // 64
+    share_rows = moment_ref.shape[0] // turns
+
+    def turn(i, carry):
+        part = pl.ds(pl.multiple_of(i * 64, 64), 64)
+        rows = pl.ds(pl.multiple_of(i * share_rows, 16), share_rows)
         precond_ref[rows, :] = 1.0 / (jnp.sqrt(moment_ref[rows, :]) + adam_epsilon)
+        signs_ref[part, :] = signs_of(col_ref[part, :], col_lanes_ref[...]).astype(jnp.bfloat16)
         return carry
 
-    lax.fori_loop(0, moment_ref.shape[0] // 32, moment_rows, 0)
+    lax.fori_loop(0, turns, turn, 0)
 
     @pl.when(step == last)
     def _():
@@ -176,7 +179,7 @@
         grad = jnp.dot(picked_ref[s], dy_ref[...], preferred_element_type=jnp.float32)
         scaled = (grad * precond_ref[...]).astype(jnp.bfloat16)
         mapped = jnp.dot(scaled, signs_ref[...], preferred_element_type=jnp.float32)
-        out_ref[s : s + 1, :] += jnp.sum(mapped * rows_ref[...], axis=0, keepdims=True)
+        out_ref[s // SEQS, s % SEQS : s % SEQS + 1, :] += jnp.sum(mapped * rows_ref[...], axis=0, keepdims=True)
 
 
 def reduce_kernel(sizes, terms_ref, out_ref, near, mine, far, near_send, near_recv, far_send, far_recv):
@@ -306,8 +309,8 @@
             pl.BlockSpec((chunk, K), lambda i: (i, 0)),
             pl.BlockSpec((rows, K), lambda i: (0, 0)),
         ],
-        out_specs=pl.BlockSpec((groups * SEQS, K), lambda i: (0, 0)),
-        out_shape=jax.ShapeDtypeStruct((groups * SEQS, K), jnp.float32),
+        out_specs=pl.BlockSpec((groups, SEQS, K), lambda i: (0, 0, 0)),
+        out_shape=jax.ShapeDtypeStruct((groups, SEQS, K), jnp.float32),
         scratch_shapes=[pltpu.VMEM((groups * SEQS, rows, count), jnp.bfloat16)],
         compiler_params=pltpu.CompilerParams(vmem_limit_bytes=58 << 20),
         cost_estimate=pl.CostEstimate(
@@ -332,7 +335,7 @@
         ],
         compiler_params=pltpu.CompilerParams(collective_id=1, has_side_effects=True),
         name="reduce",
-    )(terms.reshape(groups, SEQS, K))
+    )(terms)
 
 
 def solution(mesh):

time: 131 us -> 129 us (0.985)
  local copies, waits for them, and re-layouts: 11.3 us -> 9.98 us
    reshape x1 -> x0, local copies, waits for them, and re-layouts: 1.33 us -> none  [on_device(): terms.reshape(groups, SEQS, K)]
where the time goes in v4:
time: 129 us; the launch traced here: 128 us
  Pallas kernels  115 us (89%)
  local copies, waits for them, and re-layouts  9.98 us (8%)
  other arithmetic  2.33 us (2%)
    pallas_call x1, Pallas kernels, on_device(): pl.pallas_call(functools.partial(prepare_kernel, sizes), grid=(steps,), i...  56.3 us
    pallas_call x1, Pallas kernels, on_device(): pl.pallas_call(map_kernel, grid=(cols // chunk,), in_specs=[pl.BlockSpec(...  48.9 us
    pallas_call x1, Pallas kernels, on_device(): pl.pallas_call(functools.partial(reduce_kernel, sizes), in_specs=[pl.Bloc...  10.2 us
    unnamed x13, local copies, waits for them, and re-layouts  7.69 us

profile of v4, /device:TPU:0, one launch (start us, length us, event | category | flops | bytes accessed | tf_op | source)
XLA Modules:
  0.0 128.5 jit_solution(16631811880518247867)
XLA Ops:
  0.7 0.9 shift-right-logical_xor_fusion
  1.5 0.9 broadcast_in_dim.34.col_ref
  2.4 0.7 shift-right-logical_xor_fusion.6
  3.1 0.1 broadcast_in_dim.35.row_ref
  3.3 0.0 copy-start
  3.3 1.0 copy-done
  4.3 0.0 copy-start.1
  4.3 0.9 copy-done.1
  5.2 0.0 copy-start.2
  5.2 0.7 copy-done.2
  5.9 56.3 %prepare.1 = (bf16[8,2,16,6400]{3,2,1,0:T(8,128)(2,1)S(1)}, bf16[8,2,16,640]{3,2,1,0:T(8,128)(2,1)S(1)}, s32[2,1,128]{2,1,0:T(1,128)S(1)}, bf16[6400,1024]{1,0:T...) custom-call(bf16[16,12800]{1,0:T(8,128)(2,1)S(1)} %copy-done, bf16[4,16,640]{2,1,0:T(8,128)(2,1)S(1)} %bitcast.8, ...), custom_call_target="tpu_custom_call" | custom-call | flops 131072000 | bytes 45875200 | tf_op jit(solution)/shard_map/prepare/pallas_call | solution.py:249
  62.2 0.0 copy-start.3
  62.2 1.7 %copy-done.3 = bf16[8,2,16,6400]{3,2,1,0:T(8,128)(2,1)} copy-done((bf16[8,2,16,6400]{3,2,1,0:T(8,128)(2,1)}, bf16[8,2,16,6400]{3,2,1,0:T(8,128)(2,1)S(1)}, u32[]{:S(2)}) %copy-start.3) | copy-done | bytes 3276824
  63.9 0.0 copy-start.4
  63.9 1.5 %copy-done.4 = f32[640,1024]{1,0:T(8,128)} copy-done((f32[640,1024]{1,0:T(8,128)}, f32[640,1024]{1,0:T(8,128)S(1)}, u32[]{:S(2)}) %copy-start.4) | copy-done | bytes 2621464
  65.3 0.0 copy-start.5
  65.3 0.7 copy-done.5
  66.1 0.5 broadcast.161
  66.6 0.7 reduce.4
  67.2 0.1 reshape.118
  67.3 0.1 add_bitcast_fusion
  67.4 0.7 reshape.119.which_ref
  68.1 48.9 %map.1.terms_ref = f32[2,2,1024]{2,1,0:T(2,128)} custom-call(bf16[256,640]{1,0:T(8,128)(2,1)} %bitcast.11, s32[1,256]{1,0:T(1,128)} %reshape.119.which_ref, bf16[256,6400]{1,0:T(8,128)(2,1)} %bitcast.10, f32[640,6400]{1,0:T(8,128)} %get-tuple-element.14.precond_ref, bf16[6400,1024]{1,0:T(8,128)(2,1)} %get-tuple-element.15.signs_ref, f32[640,1024]{1,0:T(8,128)} %copy-done.4), custom_call_target="tpu_custom_call" | custom-call | flops 41943040000 | bytes 29491200 | tf_op jit(solution)/shard_map/map/pallas_call | solution.py:301
  116.9 10.2 %reduce.5 = f32[2,1024]{1,0:T(2,128)} custom-call(f32[2,2,1024]{2,1,0:T(2,128)} %map.1.terms_ref), custom_call_target="tpu_custom_call" | custom-call | tf_op jit(solution)/shard_map/reduce/pallas_call | solution.py:322
  127.2 1.3 %copy.17 = f32[2,1024]{1,0:T(2,128)} copy(f32[2,1024]{1,0:T(2,128)} %reduce.5) | data formatting | bytes 16384
  (3 shorter events, 0.0 us)
Async XLA Ops:
  3.3 1.0 copy-start
  4.3 0.9 copy-start.1
  5.2 0.7 copy-start.2
  62.2 1.7 %copy-start.3 = (bf16[8,2,16,6400]{3,2,1,0:T(8,128)(2,1)}, bf16[8,2,16,6400]{3,2,1,0:T(8,128)(2,1)S(1)}, u32[]{:S(2)}) copy-start(bf16[8,2,16,6400]{3,2,1,0:T(8,128)(2,1)S(1)} %get-tuple-element.13) | copy-start | bytes 9830404
  63.9 1.5 %copy-start.4 = (f32[640,1024]{1,0:T(8,128)}, f32[640,1024]{1,0:T(8,128)S(1)}, u32[]{:S(2)}) copy-start(f32[640,1024]{1,0:T(8,128)S(1)} %get-tuple-element.16.rows_ref) | copy-start | bytes 7864324
  65.3 0.7 copy-start.5
